TPU v7x, 32 devices: a whole 2x2x4 slice. The times are simulated.
32 devices in a mesh: groups: 2 (over x), row: 16 (over z, y, core).
Axes of the slice: x: 2, y: 2, z: 4, core: 2. Of those that a mesh axis runs over, the one named last changes fastest.
Arguments:
- panels: float32 [53248, 768], P(('groups', 'row')), parts along dimension 0, as said below
- weights: float32 [53248, 1792], P(('groups', 'row')), parts along dimension 0, may hold values from -6 to 6
- block_ids: int32 [6], P('groups'), parts along dimension 0, may hold values from 0 to 103, as said below
Outputs:
- pruned_weights: float32 [53248, 1792], P(('groups', 'row')), parts along dimension 0
- losses: float32 [6], P('groups'), parts along dimension 0
There are 2 independent parts, one for each index of `groups`. A program takes and returns all parts, laid end to end along the dimension named above; each array names one. Nothing has to cross between parts.
Inputs may be any that keep to these rules, and one draw needn't show every extreme that they name: `panels`: the columns, at the listed blocks' hidden units and in pick order, of a symmetric positive definite matrix of order 26624. `block_ids`: 3 distinct block numbers; the first and the last block of the window are always among them.
All inputs are finite; a program needn't handle non-finite values.
Results may differ from a plain program's by a relative error of at most 0.00017.
Values sent between devices are 32-bit elements; how exact they have to be, the bound alone decides.
A program may use at most 128 MiB of HBM per device.

v0:
```python
import jax
import jax.numpy as jnp
from jax import lax
from jax.sharding import PartitionSpec as P

COLS = 1792
BLOCK = 256
PICKS = 3


exact_mode = lax.Precision.HIGHEST


def chol_solve(factor, rhs):
    middle = lax.linalg.triangular_solve(factor, rhs, left_side=True, lower=True)
    return lax.linalg.triangular_solve(factor, middle, left_side=True, lower=True, transpose_a=True)


def correct(current, col_panel, diag_block, chosen, selection):
    factor = jnp.linalg.cholesky(diag_block)
    solved = chol_solve(factor, chosen)
    loss_value = jnp.sum(chosen * solved) / (2.0 * BLOCK * COLS)
    current = current - jnp.dot(col_panel, solved, precision=exact_mode)
    inside = jnp.sum(selection, axis=0) > 0.5
    current = jnp.where(inside[:, None], jnp.zeros_like(current), current)
    return (current, loss_value, factor, solved)


def body(panels, weights, block_ids):
    local_rows = panels.shape[0]
    first_row = lax.axis_index("row") * local_rows
    global_rows = first_row + jnp.arange(local_rows, dtype=jnp.int32)
    offsets = jnp.arange(BLOCK, dtype=jnp.int32)

    def selector(start_row):
        return (global_rows[None, :] == start_row + offsets[:, None]).astype(jnp.float32)

    current_panels = panels
    current = weights
    losses = []
    selections = [selector(block_ids[number] * BLOCK) for number in range(PICKS)]
    all_selection = jnp.concatenate(selections, axis=0)
    panel_terms = jnp.dot(all_selection, current_panels, precision=exact_mode)
    weight_terms = jnp.dot(all_selection, current, precision=exact_mode)
    cross, listed_weights = lax.psum((panel_terms, weight_terms), "row")
    for number in range(PICKS):
        low_edge = number * BLOCK
        col_panel = current_panels[:, low_edge : low_edge + BLOCK]
        diag_block = cross[low_edge : low_edge + BLOCK, low_edge : low_edge + BLOCK]
        chosen = listed_weights[low_edge : low_edge + BLOCK]
        current, loss_value, factor, solved = correct(
            current, col_panel, diag_block, chosen, selections[number]
        )
        losses.append(loss_value)
        if number < PICKS - 1:
            cross_cols = cross[:, low_edge : low_edge + BLOCK]
            listed_weights = listed_weights - jnp.dot(cross_cols, solved, precision=exact_mode)
            row_block = cross[low_edge : low_edge + BLOCK, :]
            left_factor = chol_solve(factor, col_panel.T).T
            current_panels = current_panels - jnp.dot(left_factor, row_block, precision=exact_mode)
            cross_left = chol_solve(factor, cross_cols.T).T
            cross = cross - jnp.dot(cross_left, row_block, precision=exact_mode)
    return (current, jnp.stack(losses))


def solution(mesh):
    in_specs = (P(("groups", "row"), None), P(("groups", "row"), None), P("groups"))
    out_specs = (P(("groups", "row"), None), P("groups"))
    return jax.shard_map(body, mesh=mesh, in_specs=in_specs, out_specs=out_specs, check_vma=False)
```

profile of v0, /device:TPU:0, one launch (start us, length us, event | category | flops | bytes accessed | tf_op | source)
XLA Modules:
  0.0 599.4 jit_solution(11035288891037630053)
XLA Ops:
  13.1 16.3 %fusion.6 = f32[768,768]{0,1:T(8,128)} fusion(f32[1664,768]{1,0:T(8,128)S(1)} %copy-done.3, f32[256,1664]{1,0:T(8,128)S(1)} %get-tuple-element.172, f32[256,1664]{1,0:T(8,128)S(1)} %get-tuple-element.171, f32[256,1664]{1,0:T(8,128)S(1)} %get-tuple-element.170), kind=kOutput, calls=%fused_computation.17 | convolution fusion | flops 11780161536 | bytes 12582912 | tf_op jit(solution)/shard_map/dot_general | solution.py:43
  29.5 33.7 %fusion.5 = f32[768,1792]{1,0:T(8,128)} fusion(f32[1664,1792]{1,0:T(8,128)S(1)} %bitcast.234, f32[256,1664]{1,0:T(8,128)S(1)} %get-tuple-element.172, f32[256,1664]{1,0:T(8,128)S(1)} %get-tuple-element.171, f32[256,1664]{1,0:T(8,128)S(1)} %get-tuple-element.170), kind=kOutput, calls=%fused_computation.16 | convolution fusion | flops 27483635712 | bytes 22544384 | tf_op jit(solution)/shard_map/dot_general | solution.py:44
  63.2 13.8 %copy.17 = f32[1664,1792]{0,1:T(8,128)} copy(f32[1664,1792]{1,0:T(8,128)} %param.17) | data formatting | bytes 23855104 | tf_op args[1]
  77.7 2.8 slice_bitcast_fusion.1
  80.5 147.7 %all-reduce.4.cloned.1.call-done = (f32[768,768]{0,1:T(8,128)}, f32[768,1792]{1,0:T(8,128)}) async-done(((f32[768,768]{0,1:T(8,128)}, f32[768,1792]{1,0:T(8,128)}), (f32[768,768]{0,1:T(8,128)}, f32[768,1792]{1,0:T(8,128)})) %all-reduce.4.cloned.1.call-update) | async-done | bytes 7864336 | tf_op jit(solution)/shard_map/psum | solution.py:45
  232.4 11.7 %cholesky.172 = f32[128,128]{1,0:T(8,128)S(1)} custom-call(f32[128,128]{1,0:T(8,128)S(1)} %cholesky.270), custom_call_target="Cholesky" | custom-call | tf_op jit(solution)/shard_map/jit(cholesky)/cholesky | solution.py:20
  244.8 9.8 %custom-call.36 = f32[1,128,128]{1,2,0:T(8,128)S(1)} custom-call(f32[1,128,128]{2,1,0:T(8,128)S(1)} %get-tuple-element.169), custom_call_target="InvertDiagBlocksLowerTriangular" | custom-call | tf_op jit(solution)/shard_map/jit(cholesky)/cholesky | solution.py:20
  255.1 11.7 %cholesky.189 = f32[128,128]{1,0:T(8,128)S(1)} custom-call(f32[128,128]{1,0:T(8,128)S(1)} %convolution_subtract_fusion.20), custom_call_target="Cholesky" | custom-call | tf_op jit(solution)/shard_map/jit(cholesky)/cholesky | solution.py:20
  268.9 4.0 while.28
  272.9 19.9 %custom-call.38 = f32[2,128,128]{1,2,0:T(8,128)S(1)} custom-call(f32[2,128,128]{2,1,0:T(8,128)S(1)} %get-tuple-element.106), custom_call_target="InvertDiagBlocksLowerTriangular" | custom-call | tf_op jit(solution)/shard_map/triangular_solve/custom-call.4 | solution.py:16
  292.8 2.3 fusion.26
  302.0 6.9 %convolution_subtract_fusion.2 = f32[768,1792]{1,0:T(8,128)} fusion(f32[768,1792]{1,0:T(8,128)S(1)} %bitcast.230, f32[128,1792]{1,0:T(8,128)S(1)} %fusion.77, f32[128,1792]{1,0:T(8,128)S(1)} %fusion.71, f32[768,768]{0,1:T(8,128)S(1)} %copy-done.6), kind=kOutput, calls=%fused_computation.15 | convolution fusion | flops 4229693440 | bytes 13631488 | tf_op jit(solution)/shard_map/dot_general | solution.py:57
  311.9 2.3 convolution_subtract_fusion.13
  317.7 11.7 %cholesky.206 = f32[128,128]{1,0:T(8,128)S(1)} custom-call(f32[128,128]{1,0:T(8,128)S(1)} %cholesky.273), custom_call_target="Cholesky" | custom-call | tf_op jit(solution)/shard_map/jit(cholesky)/cholesky | solution.py:20
  330.1 9.8 %custom-call.43 = f32[1,128,128]{1,2,0:T(8,128)S(1)} custom-call(f32[1,128,128]{2,1,0:T(8,128)S(1)} %get-tuple-element.165), custom_call_target="InvertDiagBlocksLowerTriangular" | custom-call | tf_op jit(solution)/shard_map/jit(cholesky)/cholesky | solution.py:20
  340.4 11.9 %cholesky.223 = f32[128,128]{1,0:T(8,128)S(1)} custom-call(f32[128,128]{1,0:T(8,128)S(1)} %convolution_subtract_fusion.19), custom_call_target="Cholesky" | custom-call | tf_op jit(solution)/shard_map/jit(cholesky)/cholesky | solution.py:20
  355.1 5.2 while.29
  361.0 20.5 %custom-call.45 = f32[2,128,128]{1,2,0:T(8,128)S(1)} custom-call(f32[2,128,128]{2,1,0:T(8,128)} %get-tuple-element.112), custom_call_target="InvertDiagBlocksLowerTriangular" | custom-call | tf_op jit(solution)/shard_map/triangular_solve/custom-call.4 | solution.py:16
  390.6 8.3 %convolution_subtract_fusion.1 = f32[768,1792]{1,0:T(8,128)} fusion(f32[768,1792]{1,0:T(8,128)S(1)} %bitcast.228, f32[128,1792]{1,0:T(8,128)S(1)} %fusion.86, f32[128,1792]{1,0:T(8,128)S(1)} %fusion.80, f32[768,768]{0,1:T(8,128)} %copy-done.1), kind=kOutput, calls=%fused_computation.14 | convolution fusion | flops 4229693440 | bytes 13631488 | tf_op jit(solution)/shard_map/dot_general | solution.py:57
  405.2 9.6 %convolution_subtract_fusion = f32[1664,768]{1,0:T(8,128)S(1)} fusion(f32[1664,768]{1,0:T(8,128)S(1)} %bitcast.232, f32[128,1664]{1,0:T(8,128)S(1)} %fusion.75, f32[128,1664]{1,0:T(8,128)S(1)} %fusion.70, f32[768,768]{0,1:T(8,128)} %get-tuple-element.150), kind=kOutput, calls=%fused_computation.13 | convolution fusion | flops 3927572480 | bytes 12713984 | tf_op jit(solution)/shard_map/dot_general | solution.py:60
  416.2 13.3 %fusion.18 = f32[1664,1792]{0,1:T(8,128)} fusion(f32[1664,768]{1,0:T(8,128)S(1)} %convolution_subtract_fusion, f32[128,1792]{1,0:T(8,128)S(1)} %fusion.86, f32[128,1792]{1,0:T(8,128)S(1)} %fusion.80), kind=kOutput, calls=%fused_computation.51 | convolution fusion | flops 9160818688 | bytes 15466496 | tf_op jit(solution)/shard_map/dot_general | solution.py:23
  429.6 24.0 %fusion.20 = f32[1792,1664]{1,0:T(8,128)} fusion(f32[1664,768]{1,0:T(8,128)S(1)} %bitcast.232, f32[128,1792]{1,0:T(8,128)S(1)} %fusion.77, f32[128,1792]{1,0:T(8,128)S(1)} %fusion.71), kind=kOutput, calls=%fused_computation.54 | convolution fusion | flops 9160818688 | bytes 15466496 | tf_op jit(solution)/shard_map/dot_general | solution.py:23
  460.1 11.7 %cholesky.240 = f32[128,128]{1,0:T(8,128)S(1)} custom-call(f32[128,128]{1,0:T(8,128)S(1)} %cholesky.276), custom_call_target="Cholesky" | custom-call | tf_op jit(solution)/shard_map/jit(cholesky)/cholesky | solution.py:20
  472.5 9.8 %custom-call.50 = f32[1,128,128]{1,2,0:T(8,128)S(1)} custom-call(f32[1,128,128]{2,1,0:T(8,128)S(1)} %get-tuple-element.161), custom_call_target="InvertDiagBlocksLowerTriangular" | custom-call | tf_op jit(solution)/shard_map/jit(cholesky)/cholesky | solution.py:20
  482.8 11.9 %cholesky.257 = f32[128,128]{1,0:T(8,128)S(1)} custom-call(f32[128,128]{1,0:T(8,128)S(1)} %convolution_subtract_fusion.18), custom_call_target="Cholesky" | custom-call | tf_op jit(solution)/shard_map/jit(cholesky)/cholesky | solution.py:20
  496.8 4.0 while.30
  500.9 19.7 %custom-call.52 = f32[2,128,128]{1,2,0:T(8,128)S(1)} custom-call(f32[2,128,128]{2,1,0:T(8,128)S(1)} %get-tuple-element.118), custom_call_target="InvertDiagBlocksLowerTriangular" | custom-call | tf_op jit(solution)/shard_map/triangular_solve/custom-call.4 | solution.py:16
  530.3 2.6 fusion.7
  535.6 2.7 convolution_subtract_fusion.4
  542.7 11.1 %fusion.14 = f32[1664,768]{1,0:T(8,128)} fusion(f32[128,1664]{1,0:T(8,128)S(1)} %fusion.84, f32[128,1664]{1,0:T(8,128)S(1)} %fusion.79, f32[768,768]{0,1:T(8,128)S(1)} %copy-done.2), kind=kOutput, calls=%fused_computation.42 | convolution fusion | flops 3926294528 | bytes 7602176 | tf_op jit(solution)/shard_map/dot_general | solution.py:60
  553.8 24.3 %fusion.4 = f32[1664,1792]{0,1:T(8,128)} fusion(f32[1664,1792]{0,1:T(8,128)} %fusion.18, f32[1664,1792]{0,1:T(8,128)} %copy.17, f32[1792,1664]{1,0:T(8,128)} %fusion.20, pred[1664]{0:T(1024)(128)(4,1)S(1)} %broadcast_compare_fusion, pred[1664]{0:T(1024)(128)(4,1)S(1)} %broadcast_compare_fusion.1, pred[1664]{0:T(1024)(128)(4,1)S(1)} %broadcast_compare_fusion.2, ...), kind=kOutput, calls=%fused_computation.11 | convolution fusion | flops 9179136000 | bytes 52958080 | tf_op jit(solution)/shard_map/dot_general | solution.py:23
  578.1 13.5 %copy.24 = f32[1664,1792]{1,0:T(8,128)} copy(f32[1664,1792]{0,1:T(8,128)} %fusion.4) | data formatting | bytes 23855104
  (167 shorter events, 81.0 us)
Async XLA Ops:
  7.2 221.1 %all-reduce.4.cloned.1.call-start = ((), (), s32[]{:S(2)}) async-start(), calls=%async_computation | async-start | bytes 15728640 | tf_op jit(solution)/shard_map/psum | solution.py:45
  10.7 2.5 copy-start.3
  10.7 18.8 %slice-start.6 = ((s8[11927552]{0:T(1024)(128)(4,1)}), s8[4194304]{0:T(1024)(128)(4,1)S(1)}, s32[]{:S(2)}) async-start(s8[11927552]{0:T(1024)(128)(4,1)} %bitcast.233), calls=%async_computation.7 | async-start | bytes 8388608
  13.1 16.4 %slice-start.7 = ((s8[11927552]{0:T(1024)(128)(4,1)}), s8[4194304]{0:T(1024)(128)(4,1)S(1)}, s32[]{:S(2)}) async-start(s8[11927552]{0:T(1024)(128)(4,1)} %bitcast.233), calls=%async_computation.8 | async-start | bytes 8388608
  13.1 16.4 %slice-start.8 = ((s8[11927552]{0:T(1024)(128)(4,1)}), s8[3538944]{0:T(1024)(128)(4,1)S(1)}, s32[]{:S(2)}) async-start(s8[11927552]{0:T(1024)(128)(4,1)} %bitcast.233), calls=%async_computation.9 | async-start | bytes 7077888
  272.9 38.0 %copy-start.9 = (f32[256,256]{1,0:T(8,128)}, f32[256,256]{1,0:T(8,128)S(1)}, u32[]{:S(2)}) copy-start(f32[256,256]{1,0:T(8,128)S(1)} %get-tuple-element.326) | copy-start | bytes 786436
  292.8 8.1 %slice-start.2 = ((s8[5505024]{0:T(1024)(128)(4,1)}), s8[4194304]{0:T(1024)(128)(4,1)S(1)}, s32[]{:S(2)}) async-start(s8[5505024]{0:T(1024)(128)(4,1)} %bitcast.229), calls=%async_computation.3 | async-start | bytes 8388608
  297.1 3.7 slice-start.3
  299.9 2.0 copy-start.6
  302.0 6.9 %copy-start.12 = (f32[256,768]{1,0:T(8,128)S(1)}, f32[256,768]{1,0:T(8,128)}, u32[]{:S(2)}) copy-start(f32[256,768]{1,0:T(8,128)} %slice_bitcast_fusion.3) | copy-start | bytes 2359300
  314.2 1.4 copy-start.1
  355.1 34.4 %slice-start = ((s8[5505024]{0:T(1024)(128)(4,1)}), s8[1310720]{0:T(1024)(128)(4,1)S(1)}, s32[]{:S(2)}) async-start(s8[5505024]{0:T(1024)(128)(4,1)} %bitcast.227), calls=%async_computation.1 | async-start | bytes 2621440
  360.3 0.7 copy-start.7
  383.6 4.0 copy-start.8
  385.8 3.7 slice-start.1
  389.5 15.6 %slice-start.4 = ((s8[5111808]{0:T(1024)(128)(4,1)}), s8[4194304]{0:T(1024)(128)(4,1)S(1)}, s32[]{:S(2)}) async-start(s8[5111808]{0:T(1024)(128)(4,1)} %bitcast.231), calls=%async_computation.5 | async-start | bytes 8388608
  390.6 8.3 %copy-start.5 = (f32[256,1664]{0,1:T(8,128)S(1)}, f32[256,1664]{0,1:T(8,128)}, u32[]{:S(2)}) copy-start(f32[256,1664]{0,1:T(8,128)} %slice_bitcast_fusion.1) | copy-start | bytes 5111812
  390.6 9.2 %copy-start.10 = (f32[256,256]{1,0:T(8,128)S(1)}, f32[256,256]{1,0:T(8,128)}, u32[]{:S(2)}) copy-start(f32[256,256]{1,0:T(8,128)} %copy-done.9) | copy-start | bytes 786436
  390.6 14.5 %slice-start.5 = ((s8[5111808]{0:T(1024)(128)(4,1)}), s8[917504]{0:T(1024)(128)(4,1)S(1)}, s32[]{:S(2)}) async-start(s8[5111808]{0:T(1024)(128)(4,1)} %bitcast.231), calls=%async_computation.6 | async-start | bytes 1835008
  414.8 14.8 %copy-start = (f32[1664,768]{1,0:T(8,128)}, f32[1664,768]{1,0:T(8,128)S(1)}, u32[]{:S(2)}) copy-start(f32[1664,768]{1,0:T(8,128)S(1)} %convolution_subtract_fusion) | copy-start | bytes 15335428
  429.6 24.0 %copy-start.11 = (f32[256,768]{1,0:T(8,128)S(1)}, f32[256,768]{1,0:T(8,128)}, u32[]{:S(2)}) copy-start(f32[256,768]{1,0:T(8,128)} %slice_bitcast_fusion.2) | copy-start | bytes 2359300
  454.1 3.7 copy-start.2
  500.9 19.7 %copy-start.13 = (f32[256,256]{1,0:T(8,128)}, f32[256,256]{1,0:T(8,128)S(1)}, u32[]{:S(2)}) copy-start(f32[256,256]{1,0:T(8,128)S(1)} %get-tuple-element.328) | copy-start | bytes 786436
  529.4 0.9 copy-start.4
Sparse Core Ops, SparseCore 0:
  63.4 164.8 all-reduce.3
where the time goes:
time: 609 us; the launch traced here: 599 us
  matrix products  199 us (33%)
  other arithmetic  173 us (28%)
  waiting for transfers between devices  148 us (24%)
  local copies, waits for them, and re-layouts  56.4 us (9%)
  between operations  23.1 us (4%)
    psum x1, waiting for transfers between devices, body(): cross, listed_weights = lax.psum((panel_terms, weight_terms), 'row')  148 us
    another operation x21, other arithmetic, correct(): factor = jnp.linalg.cholesky(diag_block)  104 us
    dot_general x3, matrix products, correct(): current = current - jnp.dot(col_panel, solved, precision=exact_mode)  61.6 us
    another operation x7, other arithmetic, chol_solve(): lax.linalg.triangular_solve(factor, middle, left_side=True, lower=True, t...  60.1 us
    dot_general x1, matrix products, body(): weight_terms = jnp.dot(all_selection, current, precision=exact_mode)  33.7 us
    unnamed x48, local copies, waits for them, and re-layouts  32.4 us
    another operation x21, matrix products, chol_solve(): lax.linalg.triangular_solve(factor, rhs, left_side=True, lower=True)  28 us
    dot_general x2, matrix products, body(): jnp.dot(left_factor, row_block, precision=exact_mode)  20.8 us
  transfers between devices with their start and end apart: 1, of which 1 were waited for; matrix products, arithmetic and copies ran while one was open for 3% of the time, Pallas kernels for 0%

commit v1 on v0

v1 whole, which is shorter than its diff:
```python
import jax
import jax.numpy as jnp
from jax import lax
from jax.experimental import pallas as pl
from jax.experimental.pallas import tpu as pltpu
from jax.sharding import PartitionSpec as P

BLOCK = 256
TILE = 128
exact_mode = lax.Precision.HIGHEST
split_mode = lax.Precision.HIGH


def dot_nt(a, b):
    return lax.dot_general(a, b, (((1,), (1,)), ((), ())), precision=exact_mode,
                           preferred_element_type=jnp.float32)


def dot_nn(a, b):
    return lax.dot_general(a, b, (((1,), (0,)), ((), ())), precision=exact_mode,
                           preferred_element_type=jnp.float32)


def factor_tile(tile):
    n = TILE
    groups = n // 8
    rows = lax.broadcasted_iota(jnp.int32, (8, n), 0)
    lanes = lax.broadcasted_iota(jnp.int32, (8, n), 1)
    left = [tile[8 * g : 8 * g + 8, :] for g in range(groups)]
    right = [jnp.where(lanes == rows + 8 * g, 1.0, 0.0) for g in range(groups)]
    done = []
    for j in range(0, n, 2):
        g, o = j // 8, j % 8
        c0 = {i: jnp.broadcast_to(left[i][:, j : j + 1], (8, n)) for i in range(g, groups)}
        c1 = {i: jnp.broadcast_to(left[i][:, j + 1 : j + 2], (8, n)) for i in range(g, groups)}
        a = c0[g][o : o + 1]
        b = c0[g][o + 1 : o + 2]
        d = c1[g][o + 1 : o + 2]
        inv_det = 1.0 / (a * d - b * b)
        m00, m01, m11 = d * inv_det, -b * inv_det, a * inv_det
        r0, r1 = left[g][o : o + 1], left[g][o + 1 : o + 2]
        s0, s1 = right[g][o : o + 1], right[g][o + 1 : o + 2]
        q0, q1 = m00 * r0 + m01 * r1, m01 * r0 + m11 * r1
        t0, t1 = m00 * s0 + m01 * s1, m01 * s0 + m11 * s1
        ratio = b / a
        done.append(s0 * lax.rsqrt(a))
        done.append((s1 - ratio * s0) * lax.rsqrt(d - b * ratio))
        for i in range(g, groups):
            k0, k1 = c0[i], c1[i]
            if i == g:
                if o == 6:
                    continue
                keep = rows > o + 1
                k0, k1 = jnp.where(keep, k0, 0.0), jnp.where(keep, k1, 0.0)
            left[i] = left[i] - (k0 * q0 + k1 * q1)
            right[i] = right[i] - (k0 * t0 + k1 * t1)
    return jnp.concatenate(done, axis=0)


def invert_kernel(c_ref, z_ref, m_ref, p_ref):
    n = c_ref.shape[0]
    m_ref[...] = c_ref[...]
    z_ref[...] = jnp.where(
        lax.broadcasted_iota(jnp.int32, (n, n), 0) == lax.broadcasted_iota(jnp.int32, (n, n), 1), 1.0, 0.0)

    def step(k, carry):
        here = pl.ds(pl.multiple_of(k * TILE, TILE), TILE)
        inv = factor_tile(m_ref[here, here])
        below = lax.broadcasted_iota(jnp.int32, (n, TILE), 0) >= (k + 1) * TILE
        p_ref[...] = jnp.where(below, dot_nt(m_ref[:, here], inv), 0.0)
        z_ref[here, :] = dot_nn(inv, z_ref[here, :])
        panel = p_ref[...]
        for part in range(0, n, BLOCK):
            cut = slice(part, part + BLOCK)
            m_ref[:, cut] = m_ref[:, cut] - dot_nt(panel, p_ref[cut, :])
            z_ref[:, cut] = z_ref[:, cut] - dot_nn(panel, z_ref[here, cut])
        return carry

    lax.fori_loop(0, n // TILE, step, 0)


def inverse_factor(cross):
    n = cross.shape[0]
    return pl.pallas_call(
        invert_kernel,
        out_shape=jax.ShapeDtypeStruct((n, n), jnp.float32),
        in_specs=[pl.BlockSpec(memory_space=pltpu.VMEM)],
        out_specs=pl.BlockSpec(memory_space=pltpu.VMEM),
        scratch_shapes=[pltpu.VMEM((n, n), jnp.float32), pltpu.VMEM((n, TILE), jnp.float32)],
        compiler_params=pltpu.CompilerParams(vmem_limit_bytes=32 * 1024 * 1024),
        cost_estimate=pl.CostEstimate(flops=40_000_000_000, bytes_accessed=8 * n * n, transcendentals=0),
    )(cross)


def own_rows(array, start):
    rows = array.shape[0]
    inside = jnp.clip(start, 0, rows - BLOCK)
    part = lax.dynamic_slice_in_dim(array, inside, BLOCK, 0)
    blank = jnp.zeros_like(part)
    shift = jnp.clip(start - inside, -BLOCK, BLOCK)
    return lax.dynamic_slice_in_dim(jnp.concatenate([blank, part, blank], axis=0), BLOCK + shift, BLOCK, 0)


def body(panels, weights, block_ids):
    local_rows = panels.shape[0]
    picks = block_ids.shape[0]
    cols = weights.shape[1]
    first_row = lax.axis_index("row") * local_rows
    starts = [block_ids[k] * BLOCK - first_row for k in range(picks)]

    pieces = []
    for k in range(picks):
        taken = own_rows(panels, starts[k])
        pieces += [taken[:, j * BLOCK : (j + 1) * BLOCK] for j in range(k + 1)]
    pieces = lax.psum(jnp.concatenate(pieces, axis=0), "row")
    listed = jnp.concatenate([own_rows(weights, starts[k]) for k in range(picks)], axis=0)
    pieces, listed = lax.optimization_barrier((pieces, listed))
    listed = lax.psum(listed, "row")

    def piece(i, j):
        if i < j:
            return piece(j, i).T
        at = (i * (i + 1) // 2 + j) * BLOCK
        return pieces[at : at + BLOCK]

    cross = jnp.concatenate(
        [jnp.concatenate([piece(i, j) for j in range(picks)], axis=1) for i in range(picks)], axis=0)
    inverse = inverse_factor(cross)
    left = lax.dot_general(panels, inverse, (((1,), (1,)), ((), ())), precision=split_mode)
    middle = jnp.dot(inverse, listed, precision=split_mode)
    losses = jnp.sum((middle * middle).reshape(picks, -1), axis=1) / (BLOCK * cols * 2.0)
    local = jnp.arange(local_rows, dtype=jnp.int32)
    keep = jnp.ones((local_rows,), jnp.bool_)
    for start in starts:
        keep = keep & ((local < start) | (local >= start + BLOCK))
    update = weights - jnp.dot(left, middle, precision=split_mode)
    return (jnp.where(keep[:, None], update, 0.0), losses)


def solution(mesh):
    in_specs = (P(("groups", "row"), None), P(("groups", "row"), None), P("groups"))
    out_specs = (P(("groups", "row"), None), P("groups"))
    return jax.shard_map(body, mesh=mesh, in_specs=in_specs, out_specs=out_specs, check_vma=False)
```

time: 609 us -> 291 us (0.48); the launches traced: 599 us -> 291 us
  other arithmetic: 173 us -> 12.1 us
  matrix products: 199 us -> 44.8 us
  Pallas kernels: 0 us -> 66.6 us
  local copies, waits for them, and re-layouts: 56.4 us -> 14.1 us
  waiting for transfers between devices: 148 us -> 137 us
  between operations: 23.1 us -> 16.2 us
    another operation x29 -> x0, other arithmetic: 165 us -> none  [the longest x21 104 us: correct(): factor = jnp.linalg.cholesky(diag_block)]
    dot_general x11 -> x3, matrix products: 152 us -> 44.8 us  [the longest x1 24.7 us: body(): update = weights - jnp.dot(left, middle, precision=split_mode)]
    pallas_call x0 -> x1, Pallas kernels: none -> 66.6 us  [inverse_factor(): pl.pallas_call(invert_kernel, out_shape=jax.ShapeDtypeStruct((n, n), jnp....]
    another operation x48 -> x0, matrix products: 47.3 us -> none  [the longest x21 28 us: chol_solve(): lax.linalg.triangular_solve(factor, rhs, left_side=True, lower=True)]
    unnamed x48 -> x16, local copies, waits for them, and re-layouts: 32.4 us -> 3.69 us
    another operation x28 -> x2, local copies, waits for them, and re-layouts: 14 us -> 0.17 us  [the longest x22 13.9 us: chol_solve(): lax.linalg.triangular_solve(factor, middle, left_side=True, lower=True, t...]
    psum x1 -> x2, waiting for transfers between devices: 148 us -> 137 us  [the longest x1 85.6 us: body(): pieces = lax.psum(jnp.concatenate(pieces, axis=0), 'row')]
    concatenate x0 -> x5, other arithmetic: none -> 10.6 us  [the longest x2 6.07 us: own_rows(): jnp.concatenate([blank, part, blank], axis=0)]
  transfers between devices with their start and end apart: 1 -> 2, of which waited for: 1 -> 2; matrix products, arithmetic and copies ran while one was open for 3% -> 7% of each run, Pallas kernels for 0% -> 23%
where the time goes in v1:
time: 291 us
  waiting for transfers between devices  137 us (47%)
  Pallas kernels  66.6 us (23%)
  matrix products  44.8 us (15%)
  between operations  16.2 us (6%)
  local copies, waits for them, and re-layouts  14.1 us (5%)
  other arithmetic  12.1 us (4%)
    psum x1, waiting for transfers between devices, body(): pieces = lax.psum(jnp.concatenate(pieces, axis=0), 'row')  85.6 us
    pallas_call x1, Pallas kernels, inverse_factor(): pl.pallas_call(invert_kernel, out_shape=jax.ShapeDtypeStruct((n, n), jnp....  66.6 us
    psum x1, waiting for transfers between devices, body(): listed = lax.psum(listed, 'row')  51.5 us
    dot_general x1, matrix products, body(): update = weights - jnp.dot(left, middle, precision=split_mode)  24.7 us
    dot_general x1, matrix products, body(): middle = jnp.dot(inverse, listed, precision=split_mode)  11.6 us
    dot_general x1, matrix products, body(): lax.dot_general(panels, inverse, (((1,), (1,)), ((), ())), precision=spli...  8.47 us
    concatenate x2, other arithmetic, own_rows(): jnp.concatenate([blank, part, blank], axis=0)  6.07 us
  transfers between devices with their start and end apart: 2, of which 2 were waited for; matrix products, arithmetic and copies ran while one was open for 7% of the time, Pallas kernels for 23%

profile of v1, /device:TPU:0, one launch (start us, length us, event | category | flops | bytes accessed | tf_op | source)
XLA Modules:
  0.0 291.0 jit_solution(14323540698425431119)
XLA Ops:
  7.2 0.0 all-reduce.3.cloned.1.call-start
  7.2 1.4 fusion.19
  10.6 1.9 constant_dynamic-slice_fusion.3
  12.4 0.1 broadcast.34
  12.5 0.9 fusion.12
  13.4 1.1 fusion.7
  14.5 0.7 slice_dynamic-update-slice_fusion.4
  15.3 0.7 slice_dynamic-update-slice_fusion.3
  16.0 0.7 slice_dynamic-update-slice_fusion.2
  16.7 0.7 slice_dynamic-update-slice_fusion.1
  17.4 0.7 slice_dynamic-update-slice_fusion
  18.2 0.0 all-reduce.5.cloned.1.call-start
  18.2 3.1 %constant_dynamic-slice_fusion.2 = (f32[256,1792]{1,0:T(8,128)S(1)}, f32[256,1792]{1,0:T(8,128)S(1)}, f32[256,1792]{1,0:T(8,128)S(1)}) fusion(f32[1664,1792]{1,0:T(8,128)} %param.4, s32[]{:T(128)S(6)} %min.25, s32[]{:T(128)S(6)} %min.27, s32[]{:T(128)S(6)} %min.29), kind=kLoop, calls=%fused_computation.54 | loop fusion | bytes 11010060 | tf_op jit(solution)/shard_map/dynamic_slice | solution.py:98
  21.4 0.1 broadcast.35
  21.5 5.0 %fusion.5 = (f32[256,1792]{1,0:T(8,128)S(1)}, f32[256,1792]{1,0:T(8,128)S(1)}, f32[256,1792]{1,0:T(8,128)}) fusion(s32[]{:T(128)S(6)} %select_n.9, f32[256,1792]{1,0:T(8,128)S(1)} %get-tuple-element.6, f32[256,1792]{1,0:T(8,128)S(1)} %broadcast.35, s32[]{:T(128)S(6)} %select_n.11, f32[256,1792]{1,0:T(8,128)S(1)} %get-tuple-element.8, s32[]{:T(128)S(6)} %select_n.10, ...), kind=kLoop, calls=%fused_computation.27 | loop fusion | flops 2752512 | bytes 12845068 | tf_op jit(solution)/shard_map/concatenate | solution.py:101
  26.5 4.3 %pad_maximum_fusion = f32[768,1792]{1,0:T(8,128)} fusion(f32[256,1792]{1,0:T(8,128)S(1)} %get-tuple-element.13, f32[256,1792]{1,0:T(8,128)} %get-tuple-element.14, f32[256,1792]{1,0:T(8,128)S(1)} %get-tuple-element.12), kind=kLoop, calls=%fused_computation.10 | loop fusion | flops 2752512 | bytes 11010048 | tf_op jit(solution)/shard_map/concatenate | solution.py:116
  30.8 85.6 %all-reduce.3.cloned.1.call-done = f32[1536,256]{1,0:T(8,128)} async-done(((f32[1536,256]{1,0:T(8,128)}), f32[1536,256]{1,0:T(8,128)}) %all-reduce.3.cloned.1.call-update) | async-done | bytes 1572880 | tf_op jit(solution)/shard_map/psum | solution.py:115
  116.4 2.2 fusion.18
  118.5 0.5 copy.10
  119.1 0.1 slice_bitcast_fusion.1
  119.2 0.8 copy-done.3
  120.0 0.1 pad_maximum_fusion.1
  120.0 0.3 copy.14
  120.3 0.1 copy.13
  120.5 0.2 maximum_maximum_fusion.c_ref
  120.6 66.6 %shard_map.50 = f32[768,768]{1,0:T(8,128)S(1)} custom-call(f32[768,768]{1,0:T(8,128)S(1)} %maximum_maximum_fusion.c_ref), custom_call_target="tpu_custom_call" | custom-call | flops 40000000000 | bytes 4718592 | tf_op jit(solution)/shard_map/pallas_call | solution.py:84
  187.3 8.5 %fusion.20 = f32[768,1664]{1,0:T(8,128)} fusion(f32[768,768]{1,0:T(8,128)S(1)} %shard_map.50, f32[1664,768]{1,0:T(8,128)S(1)} %bitcast.16), kind=kOutput, calls=%fused_computation.64 | convolution fusion | flops 5888802816 | bytes 12582912 | tf_op jit(solution)/shard_map/dot_general | solution.py:129
  195.7 51.5 %all-reduce.5.cloned.1.call-done = f32[768,1792]{1,0:T(8,128)} async-done(((f32[768,1792]{1,0:T(8,128)}), f32[768,1792]{1,0:T(8,128)}) %all-reduce.5.cloned.1.call-update) | async-done | bytes 5505040 | tf_op jit(solution)/shard_map/psum | solution.py:118
  247.2 11.6 %multiply_reduce_fusion = (f32[768]{0:T(1024)S(1)}, f32[768,1792]{1,0:T(8,128)}) fusion(f32[768,768]{1,0:T(8,128)S(1)} %shard_map.50, f32[768,1792]{1,0:T(8,128)} %all-reduce.5.cloned.1.call-done), kind=kOutput, calls=%fused_computation.11 | convolution fusion | flops 6344539136 | bytes 13372416 | tf_op jit(solution)/shard_map/dot_general | solution.py:130
  258.8 0.1 reduce_sum.18
  259.0 0.5 broadcast_multiply_fusion
  259.5 24.7 %subtract_select_fusion = f32[1664,1792]{1,0:T(8,128)} fusion(f32[1664,1792]{1,0:T(8,128)} %param.4, f32[768,1664]{1,0:T(8,128)} %fusion.20, f32[768,1792]{1,0:T(8,128)} %get-tuple-element.30, pred[1664]{0:T(1024)(128)(4,1)S(1)} %fusion.15), kind=kOutput, calls=%fused_computation | convolution fusion | flops 13746503680 | bytes 34473600 | tf_op jit(solution)/shard_map/dot_general | solution.py:136
  (16 shorter events, 0.1 us)
Async XLA Ops:
  7.2 109.2 %all-reduce.3.cloned.1.call-start = ((), (), s32[]{:S(2)}) async-start(), calls=%async_computation | async-start | bytes 3145728 | tf_op jit(solution)/shard_map/psum | solution.py:115
  18.2 229.1 %all-reduce.5.cloned.1.call-start = ((), (), s32[]{:S(2)}) async-start(), calls=%async_computation.1 | async-start | bytes 11010048 | tf_op jit(solution)/shard_map/psum | solution.py:118
  116.4 2.2 copy-start
  119.0 1.0 copy-start.3
  119.2 1.3 copy-start.1
  119.2 1.3 copy-start.2
  120.5 66.8 %slice-start = ((s8[5111808]{0:T(1024)(128)(4,1)}), s8[4194304]{0:T(1024)(128)(4,1)S(1)}, s32[]{:S(2)}) async-start(s8[5111808]{0:T(1024)(128)(4,1)} %bitcast.15), calls=%async_computation.2 | async-start | bytes 8388608
  120.6 66.6 %slice-start.1 = ((s8[5111808]{0:T(1024)(128)(4,1)}), s8[917504]{0:T(1024)(128)(4,1)S(1)}, s32[]{:S(2)}) async-start(s8[5111808]{0:T(1024)(128)(4,1)} %bitcast.15), calls=%async_computation.3 | async-start | bytes 1835008
Sparse Core Ops, SparseCore 0:
  18.3 98.0 all-reduce.2
  120.6 126.5 all-reduce.4

commit v2 on v1

--- a/solution.py
+++ b/solution.py
@@ -114,7 +114,6 @@
         pieces += [taken[:, j * BLOCK : (j + 1) * BLOCK] for j in range(k + 1)]
     pieces = lax.psum(jnp.concatenate(pieces, axis=0), "row")
     listed = jnp.concatenate([own_rows(weights, starts[k]) for k in range(picks)], axis=0)
-    pieces, listed = lax.optimization_barrier((pieces, listed))
     listed = lax.psum(listed, "row")
 
     def piece(i, j):

time: 291 us -> 304 us (1.045)
  waiting for transfers between devices: 137 us -> 154 us
    psum x1, waiting for transfers between devices: 85.6 us -> 154 us  [body(): pieces = lax.psum(jnp.concatenate(pieces, axis=0), 'row')]
    psum x1 -> x0, waiting for transfers between devices: 51.5 us -> none  [body(): listed = lax.psum(listed, 'row')]
  transfers between devices with their start and end apart: 2 -> 1, of which waited for: 2 -> 1; matrix products, arithmetic and copies ran while one was open for 7% -> 0% of each run, Pallas kernels for 23% -> 0%
where the time goes in v2:
time: 304 us
  waiting for transfers between devices  154 us (51%)
  Pallas kernels  66.6 us (22%)
  matrix products  42.9 us (14%)
  between operations  16.2 us (5%)
  local copies, waits for them, and re-layouts  12.3 us (4%)
  other arithmetic  12.2 us (4%)
    psum x1, waiting for transfers between devices, body(): pieces = lax.psum(jnp.concatenate(pieces, axis=0), 'row')  154 us
    pallas_call x1, Pallas kernels, inverse_factor(): pl.pallas_call(invert_kernel, out_shape=jax.ShapeDtypeStruct((n, n), jnp....  66.6 us
    dot_general x1, matrix products, body(): update = weights - jnp.dot(left, middle, precision=split_mode)  24.7 us
    dot_general x1, matrix products, body(): middle = jnp.dot(inverse, listed, precision=split_mode)  9.6 us
    dot_general x1, matrix products, body(): lax.dot_general(panels, inverse, (((1,), (1,)), ((), ())), precision=spli...  8.57 us
    concatenate x2, other arithmetic, own_rows(): jnp.concatenate([blank, part, blank], axis=0)  6.11 us
  transfers between devices with their start and end apart: 1, of which 1 were waited for; matrix products, arithmetic and copies ran while one was open for 0% of the time, Pallas kernels for 0%

profile of v2, /device:TPU:0, one launch (start us, length us, event | category | flops | bytes accessed | tf_op | source)
XLA Modules:
  0.0 303.8 jit_solution(14384059569303187542)
XLA Ops:
  7.2 0.0 all-reduce.3.cloned.1.call-start
  7.2 1.4 fusion.19
  10.6 1.8 constant_dynamic-slice_fusion.3
  12.5 0.1 broadcast.34
  12.5 0.9 fusion.12
  13.4 1.1 fusion.7
  14.6 0.7 slice_dynamic-update-slice_fusion.4
  15.3 0.7 slice_dynamic-update-slice_fusion.3
  16.0 0.7 slice_dynamic-update-slice_fusion.2
  16.7 0.8 slice_dynamic-update-slice_fusion.1
  17.5 0.7 slice_dynamic-update-slice_fusion
  18.2 3.1 %constant_dynamic-slice_fusion.2 = (f32[256,1792]{1,0:T(8,128)S(1)}, f32[256,1792]{1,0:T(8,128)S(1)}, f32[256,1792]{1,0:T(8,128)S(1)}) fusion(f32[1664,1792]{1,0:T(8,128)} %param.4, s32[]{:T(128)S(6)} %min.25, s32[]{:T(128)S(6)} %min.27, s32[]{:T(128)S(6)} %min.29), kind=kLoop, calls=%fused_computation.54 | loop fusion | bytes 11010060 | tf_op jit(solution)/shard_map/dynamic_slice | solution.py:98
  21.3 0.1 broadcast.35
  21.4 5.0 %fusion.5 = (f32[256,1792]{1,0:T(8,128)S(1)}, f32[256,1792]{1,0:T(8,128)S(1)}, f32[256,1792]{1,0:T(8,128)}) fusion(s32[]{:T(128)S(6)} %select_n.9, f32[256,1792]{1,0:T(8,128)S(1)} %get-tuple-element.4, f32[256,1792]{1,0:T(8,128)S(1)} %broadcast.35, s32[]{:T(128)S(6)} %select_n.11, f32[256,1792]{1,0:T(8,128)S(1)} %get-tuple-element.6, s32[]{:T(128)S(6)} %select_n.10, ...), kind=kLoop, calls=%fused_computation.27 | loop fusion | flops 2752512 | bytes 12845068 | tf_op jit(solution)/shard_map/concatenate | solution.py:101
  26.4 4.3 %pad_maximum_fusion = f32[768,1792]{1,0:T(8,128)} fusion(f32[256,1792]{1,0:T(8,128)S(1)} %get-tuple-element.11, f32[256,1792]{1,0:T(8,128)} %get-tuple-element.12, f32[256,1792]{1,0:T(8,128)S(1)} %get-tuple-element.10), kind=kLoop, calls=%fused_computation.10 | loop fusion | flops 2752512 | bytes 11010048 | tf_op jit(solution)/shard_map/concatenate | solution.py:116
  30.7 0.0 all-reduce.3.cloned.1.call-update
  30.8 153.6 %all-reduce.3.cloned.1.call-done = (f32[1536,256]{1,0:T(8,128)}, f32[768,1792]{1,0:T(8,128)}) async-done(((f32[1536,256]{1,0:T(8,128)}, f32[768,1792]{1,0:T(8,128)}), (f32[1536,256]{1,0:T(8,128)}, f32[768,1792]{1,0:T(8,128)})) %all-reduce.3.cloned.1.call-update) | async-done | bytes 7077904 | tf_op jit(solution)/shard_map/psum | solution.py:115
  184.4 1.5 fusion.18
  185.9 0.1 copy.15
  186.0 0.1 copy.17
  186.1 0.1 pad_maximum_fusion.1
  186.2 0.3 copy.14
  186.5 0.1 copy.16
  186.6 0.0 slice-start
  186.6 0.2 maximum_maximum_fusion.c_ref
  186.8 0.0 slice-start.1
  186.8 66.6 %shard_map.50 = f32[768,768]{1,0:T(8,128)S(1)} custom-call(f32[768,768]{1,0:T(8,128)S(1)} %maximum_maximum_fusion.c_ref), custom_call_target="tpu_custom_call" | custom-call | flops 40000000000 | bytes 4718592 | tf_op jit(solution)/shard_map/pallas_call | solution.py:84
  253.4 8.6 %fusion.20 = f32[768,1664]{1,0:T(8,128)} fusion(f32[768,768]{1,0:T(8,128)S(1)} %shard_map.50, f32[1664,768]{1,0:T(8,128)S(1)} %bitcast.15), kind=kOutput, calls=%fused_computation.62 | convolution fusion | flops 5888802816 | bytes 12582912 | tf_op jit(solution)/shard_map/dot_general | solution.py:128
  262.0 9.6 %multiply_reduce_fusion = (f32[768]{0:T(1024)S(1)}, f32[768,1792]{1,0:T(8,128)}) fusion(f32[768,768]{1,0:T(8,128)S(1)} %shard_map.50, f32[768,1792]{1,0:T(8,128)S(1)} %bitcast.18), kind=kOutput, calls=%fused_computation.11 | convolution fusion | flops 6344539136 | bytes 13372416 | tf_op jit(solution)/shard_map/dot_general | solution.py:129
  271.6 0.1 reduce_sum.18
  271.8 0.5 broadcast_multiply_fusion
  272.3 24.7 %subtract_select_fusion = f32[1664,1792]{1,0:T(8,128)} fusion(f32[1664,1792]{1,0:T(8,128)} %param.4, f32[768,1664]{1,0:T(8,128)} %fusion.20, f32[768,1792]{1,0:T(8,128)} %get-tuple-element.26, pred[1664]{0:T(1024)(128)(4,1)S(1)} %fusion.15), kind=kOutput, calls=%fused_computation | convolution fusion | flops 13746503680 | bytes 34473600 | tf_op jit(solution)/shard_map/dot_general | solution.py:135
  (10 shorter events, 0.0 us)
Async XLA Ops:
  7.2 177.2 %all-reduce.3.cloned.1.call-start = ((), (), s32[]{:S(2)}) async-start(), calls=%async_computation | async-start | bytes 14155776 | tf_op jit(solution)/shard_map/psum | solution.py:115
  186.6 66.8 %slice-start = ((s8[5111808]{0:T(1024)(128)(4,1)}), s8[4194304]{0:T(1024)(128)(4,1)S(1)}, s32[]{:S(2)}) async-start(s8[5111808]{0:T(1024)(128)(4,1)} %bitcast.14), calls=%async_computation.1 | async-start | bytes 8388608
  186.6 75.4 %slice-start.2 = ((s8[5505024]{0:T(1024)(128)(4,1)}), s8[4194304]{0:T(1024)(128)(4,1)S(1)}, s32[]{:S(2)}) async-start(s8[5505024]{0:T(1024)(128)(4,1)} %bitcast.17), calls=%async_computation.3 | async-start | bytes 8388608
  186.8 66.6 %slice-start.1 = ((s8[5111808]{0:T(1024)(128)(4,1)}), s8[917504]{0:T(1024)(128)(4,1)S(1)}, s32[]{:S(2)}) async-start(s8[5111808]{0:T(1024)(128)(4,1)} %bitcast.14), calls=%async_computation.2 | async-start | bytes 1835008
  186.8 75.2 %slice-start.3 = ((s8[5505024]{0:T(1024)(128)(4,1)}), s8[1310720]{0:T(1024)(128)(4,1)S(1)}, s32[]{:S(2)}) async-start(s8[5505024]{0:T(1024)(128)(4,1)} %bitcast.17), calls=%async_computation.4 | async-start | bytes 2621440
Sparse Core Ops, SparseCore 0:
  30.9 153.4 all-reduce.2

commit v3 on v1

--- a/solution.py
+++ b/solution.py
@@ -1,3 +1,6 @@
+import functools
+import math
+
 import jax
 import jax.numpy as jnp
 from jax import lax
@@ -92,13 +95,102 @@
     )(cross)
 
 
-def own_rows(array, start):
-    rows = array.shape[0]
-    inside = jnp.clip(start, 0, rows - BLOCK)
-    part = lax.dynamic_slice_in_dim(array, inside, BLOCK, 0)
-    blank = jnp.zeros_like(part)
-    shift = jnp.clip(start - inside, -BLOCK, BLOCK)
-    return lax.dynamic_slice_in_dim(jnp.concatenate([blank, part, blank], axis=0), BLOCK + shift, BLOCK, 0)
+def pick_kernel(picks, chunk, tri, starts_ref, x_ref, o_ref, sems):
+    o_ref[...] = jnp.zeros_like(o_ref)
+    rows = x_ref.shape[0]
+
+    def each(act):
+        number = 0
+        for k in range(picks):
+            for c in range(BLOCK // chunk):
+                at = starts_ref[k] + c * chunk
+                copies = []
+                for j in range(k + 1 if tri else 1):
+                    place = (k * (k + 1) // 2 + j if tri else k) * BLOCK + c * chunk
+                    source = x_ref.at[pl.ds(pl.multiple_of(jnp.clip(at, 0, rows - chunk), 8), chunk)]
+                    if tri:
+                        source = source.at[:, j * BLOCK : (j + 1) * BLOCK]
+                    copies.append(pltpu.make_async_copy(source, o_ref.at[pl.ds(place, chunk)], sems.at[number]))
+                    number += 1
+
+                @pl.when((at >= 0) & (at < rows))
+                def _(copies=copies):
+                    for copy in copies:
+                        act(copy)
+
+    each(lambda copy: copy.start())
+    each(lambda copy: copy.wait())
+
+
+def pick_rows(array, starts, picks, tri):
+    rows, cols = array.shape
+    chunk = math.gcd(BLOCK, rows)
+    blocks = picks * (picks + 1) // 2 if tri else picks
+    out = (blocks * BLOCK, BLOCK if tri else cols)
+    return pl.pallas_call(
+        functools.partial(pick_kernel, picks, chunk, tri),
+        out_shape=jax.ShapeDtypeStruct(out, array.dtype),
+        in_specs=[pl.BlockSpec(memory_space=pltpu.SMEM), pl.BlockSpec(memory_space=pl.ANY)],
+        out_specs=pl.BlockSpec(memory_space=pltpu.VMEM),
+        scratch_shapes=[pltpu.SemaphoreType.DMA((blocks * (BLOCK // chunk),))],
+        compiler_params=pltpu.CompilerParams(vmem_limit_bytes=24 * 1024 * 1024),
+        cost_estimate=pl.CostEstimate(flops=0, bytes_accessed=8 * out[0] * out[1], transcendentals=0),
+    )(starts, array)
+
+
+def sum_kernel(n, x_ref, o_ref, acc, got, full, send_sems, recv_sems):
+    me = lax.axis_index("row")
+    steps = n.bit_length() - 1
+    rows = x_ref.shape[0]
+    sides = [lax.rem(me // (1 << s), 2) for s in range(steps)]
+    partners = [me + (1 << s) * (1 - 2 * sides[s]) for s in range(steps)]
+    barrier = pltpu.get_barrier_semaphore()
+    for partner in partners:
+        pl.semaphore_signal(barrier, inc=1, device_id={"row": partner}, device_id_type=pl.DeviceIdType.MESH)
+    acc[...] = x_ref[...]
+    pl.semaphore_wait(barrier, steps)
+
+    def copy(source, target, number, partner):
+        return pltpu.make_async_remote_copy(
+            src_ref=source, dst_ref=target, send_sem=send_sems.at[number], recv_sem=recv_sems.at[number],
+            device_id={"row": partner}, device_id_type=pl.DeviceIdType.MESH)
+
+    low, size, lows = 0, rows, []
+    for s in range(steps):
+        half = size // 2
+        away = pl.multiple_of(low + (1 - sides[s]) * half, 8)
+        low = pl.multiple_of(low + sides[s] * half, 8)
+        landing = pl.ds(rows - size, half)
+        sent = copy(acc.at[pl.ds(away, half)], got.at[landing], s, partners[s])
+        sent.start()
+        sent.wait()
+        acc[pl.ds(low, half), :] = acc[pl.ds(low, half), :] + got[landing, :]
+        size = half
+        lows.append(low)
+    full[pl.ds(low, size), :] = acc[pl.ds(low, size), :]
+    for s in reversed(range(steps)):
+        here = pl.ds(lows[s], size)
+        sent = copy(full.at[here], full.at[here], steps + s, partners[s])
+        sent.start()
+        sent.wait()
+        size = size * 2
+    o_ref[...] = full[...]
+
+
+def sum_rows(array, n):
+    rows, cols = array.shape
+    steps = n.bit_length() - 1
+    return pl.pallas_call(
+        functools.partial(sum_kernel, n),
+        out_shape=jax.ShapeDtypeStruct(array.shape, array.dtype),
+        in_specs=[pl.BlockSpec(memory_space=pltpu.VMEM)],
+        out_specs=pl.BlockSpec(memory_space=pltpu.VMEM),
+        scratch_shapes=[pltpu.VMEM((rows, cols), array.dtype)] * 3
+        + [pltpu.SemaphoreType.DMA((2 * steps,)), pltpu.SemaphoreType.DMA((2 * steps,))],
+        compiler_params=pltpu.CompilerParams(
+            vmem_limit_bytes=24 * 1024 * 1024, collective_id=0, has_side_effects=True),
+        cost_estimate=pl.CostEstimate(flops=40_000_000_000, bytes_accessed=8 * rows * cols, transcendentals=0),
+    )(array)
 
 
 def body(panels, weights, block_ids):
@@ -108,14 +200,12 @@
     first_row = lax.axis_index("row") * local_rows
     starts = [block_ids[k] * BLOCK - first_row for k in range(picks)]
 
-    pieces = []
-    for k in range(picks):
-        taken = own_rows(panels, starts[k])
-        pieces += [taken[:, j * BLOCK : (j + 1) * BLOCK] for j in range(k + 1)]
-    pieces = lax.psum(jnp.concatenate(pieces, axis=0), "row")
-    listed = jnp.concatenate([own_rows(weights, starts[k]) for k in range(picks)], axis=0)
+    local_starts = jnp.stack(starts)
+    pieces = pick_rows(panels, local_starts, picks, True)
+    listed = pick_rows(weights, local_starts, picks, False)
     pieces, listed = lax.optimization_barrier((pieces, listed))
     listed = lax.psum(listed, "row")
+    pieces = sum_rows(pieces, lax.axis_size("row"))
 
     def piece(i, j):
         if i < j:

time: 291 us -> 213 us (0.73)
  waiting for transfers between devices: 137 us -> 1.42 us
  Pallas kernels: 66.6 us -> 138 us
  other arithmetic: 12.1 us -> 0.94 us
    psum x1 -> x0, waiting for transfers between devices: 85.6 us -> none  [body(): pieces = lax.psum(jnp.concatenate(pieces, axis=0), 'row')]
    pallas_call x0 -> x3, Pallas kernels: none -> 70.8 us  [the longest x1 68.5 us: sum_rows(): pl.pallas_call(functools.partial(sum_kernel, n), out_shape=jax.ShapeDtype...]
    psum x1, waiting for transfers between devices: 51.5 us -> 1.4 us  [body(): listed = lax.psum(listed, 'row')]
    concatenate x3 -> x0, other arithmetic: 10.4 us -> none  [the longest x2 6.07 us: own_rows(): jnp.concatenate([blank, part, blank], axis=0)]
    unnamed x16 -> x13, local copies, waits for them, and re-layouts: 3.69 us -> 9.67 us
    dynamic_slice x2 -> x0, local copies, waits for them, and re-layouts: 4.98 us -> none  [own_rows(): part = lax.dynamic_slice_in_dim(array, inside, BLOCK, 0)]
  transfers between devices with their start and end apart: 2 -> 1, of which waited for: 2 -> 1; matrix products, arithmetic and copies ran while one was open for 7% -> 4% of each run, Pallas kernels for 23% -> 64%
where the time goes in v3:
time: 213 us; the launch traced here: 212 us
  Pallas kernels  138 us (65%)
  matrix products  44.9 us (21%)
  between operations  16.1 us (8%)
  local copies, waits for them, and re-layouts  11.4 us (5%)
    pallas_call x1, Pallas kernels, sum_rows(): pl.pallas_call(functools.partial(sum_kernel, n), out_shape=jax.ShapeDtype...  68.5 us
    pallas_call x1, Pallas kernels, inverse_factor(): pl.pallas_call(invert_kernel, out_shape=jax.ShapeDtypeStruct((n, n), jnp....  66.8 us
    dot_general x1, matrix products, body(): update = weights - jnp.dot(left, middle, precision=split_mode)  24.7 us
    dot_general x1, matrix products, body(): middle = jnp.dot(inverse, listed, precision=split_mode)  11.7 us
    unnamed x13, local copies, waits for them, and re-layouts  9.67 us
    dot_general x1, matrix products, body(): lax.dot_general(panels, inverse, (((1,), (1,)), ((), ())), precision=spli...  8.5 us
  transfers between devices with their start and end apart: 1, of which 1 were waited for; matrix products, arithmetic and copies ran while one was open for 4% of the time, Pallas kernels for 64%

profile of v3, /device:TPU:0, one launch (start us, length us, event | category | flops | bytes accessed | tf_op | source)
XLA Modules:
  0.0 212.4 jit_solution(1423049738622657867)
XLA Ops:
  7.2 0.0 all-reduce.2.cloned.1.call-start
  7.2 1.3 fusion.6
  10.4 0.1 pad_add_fusion.starts_ref
  10.5 0.0 copy-start.2
  10.5 2.4 %copy-done.2 = f32[1664,768]{1,0:T(8,128)S(1)} copy-done((f32[1664,768]{1,0:T(8,128)S(1)}, f32[1664,768]{1,0:T(8,128)}, u32[]{:S(2)}) %copy-start.2) | copy-done | bytes 5111832
  13.0 0.9 shard_map.50.x_ref
  13.8 0.0 copy-start.1
  13.9 4.4 %copy-done.1 = f32[1664,1792]{1,0:T(8,128)S(1)} copy-done((f32[1664,1792]{1,0:T(8,128)S(1)}, f32[1664,1792]{1,0:T(8,128)}, u32[]{:S(2)}) %copy-start.1) | copy-done | bytes 11927576
  18.2 1.5 shard_map.51
  19.7 0.0 copy-start
  19.7 2.4 %copy-done = f32[768,1792]{1,0:T(8,128)} copy-done((f32[768,1792]{1,0:T(8,128)}, f32[768,1792]{1,0:T(8,128)S(1)}, u32[]{:S(2)}) %copy-start) | copy-done | bytes 5505048
  22.2 0.0 all-reduce.2.cloned.1.call-update
  22.2 68.5 %shard_map.52 = f32[1536,256]{1,0:T(8,128)S(1)} custom-call(f32[1536,256]{1,0:T(8,128)S(1)} %shard_map.50.x_ref), custom_call_target="tpu_custom_call" | custom-call | flops 40000000000 | bytes 3145728 | tf_op jit(solution)/shard_map/pallas_call | solution.py:183
  90.7 0.1 fusion.5
  90.8 0.1 copy.15
  91.0 0.1 copy.17
  91.1 0.1 pad_maximum_fusion
  91.2 0.3 copy.14
  91.4 0.1 copy.16
  91.6 0.0 slice-start
  91.6 0.2 maximum_maximum_fusion.c_ref
  91.8 0.0 slice-start.1
  91.8 66.8 %shard_map.53 = f32[768,768]{1,0:T(8,128)S(1)} custom-call(f32[768,768]{1,0:T(8,128)S(1)} %maximum_maximum_fusion.c_ref), custom_call_target="tpu_custom_call" | custom-call | flops 40000000000 | bytes 4718592 | tf_op jit(solution)/shard_map/pallas_call | solution.py:87
  158.6 0.0 slice-done
  158.6 0.0 slice-done.1
  158.6 8.5 %fusion.7 = f32[768,1664]{1,0:T(8,128)} fusion(f32[768,768]{1,0:T(8,128)S(1)} %shard_map.53, f32[1664,768]{1,0:T(8,128)S(1)} %bitcast.17), kind=kOutput, calls=%fused_computation.20 | convolution fusion | flops 5888802816 | bytes 12582912 | tf_op jit(solution)/shard_map/dot_general | solution.py:219
  167.1 1.4 all-reduce.2.cloned.1.call-done
  168.5 11.7 %multiply_reduce_fusion = (f32[768]{0:T(1024)S(1)}, f32[768,1792]{1,0:T(8,128)}) fusion(f32[768,768]{1,0:T(8,128)S(1)} %shard_map.53, f32[768,1792]{1,0:T(8,128)} %all-reduce.2.cloned.1.call-done), kind=kOutput, calls=%fused_computation.1 | convolution fusion | flops 6344539136 | bytes 13372416 | tf_op jit(solution)/shard_map/dot_general | solution.py:220
  180.2 0.1 reduce_sum.18
  180.3 0.5 broadcast_multiply_fusion
  180.8 24.7 %subtract_select_fusion = f32[1664,1792]{1,0:T(8,128)} fusion(f32[1664,1792]{1,0:T(8,128)} %x_ref.3, f32[768,1664]{1,0:T(8,128)} %fusion.7, f32[768,1792]{1,0:T(8,128)} %get-tuple-element.17, pred[1664]{0:T(1024)(128)(4,1)S(1)} %fusion.2), kind=kOutput, calls=%fused_computation | convolution fusion | flops 13746503680 | bytes 34473600 | tf_op jit(solution)/shard_map/dot_general | solution.py:226
  (3 shorter events, 0.0 us)
Async XLA Ops:
  7.2 161.3 %all-reduce.2.cloned.1.call-start = ((), (), s32[]{:S(2)}) async-start(), calls=%async_computation | async-start | bytes 11010048 | tf_op jit(solution)/shard_map/psum | solution.py:207
  10.5 2.5 %copy-start.2 = (f32[1664,768]{1,0:T(8,128)S(1)}, f32[1664,768]{1,0:T(8,128)}, u32[]{:S(2)}) copy-start(f32[1664,768]{1,0:T(8,128)} %x_ref.2) | copy-start | bytes 15335428
  13.8 4.4 %copy-start.1 = (f32[1664,1792]{1,0:T(8,128)S(1)}, f32[1664,1792]{1,0:T(8,128)}, u32[]{:S(2)}) copy-start(f32[1664,1792]{1,0:T(8,128)} %x_ref.3) | copy-start | bytes 35782660
  19.7 2.4 %copy-start = (f32[768,1792]{1,0:T(8,128)}, f32[768,1792]{1,0:T(8,128)S(1)}, u32[]{:S(2)}) copy-start(f32[768,1792]{1,0:T(8,128)S(1)} %shard_map.51) | copy-start | bytes 16515076
  91.6 67.0 %slice-start = ((s8[5111808]{0:T(1024)(128)(4,1)}), s8[4194304]{0:T(1024)(128)(4,1)S(1)}, s32[]{:S(2)}) async-start(s8[5111808]{0:T(1024)(128)(4,1)} %bitcast.16), calls=%async_computation.1 | async-start | bytes 8388608
  91.8 66.8 %slice-start.1 = ((s8[5111808]{0:T(1024)(128)(4,1)}), s8[917504]{0:T(1024)(128)(4,1)S(1)}, s32[]{:S(2)}) async-start(s8[5111808]{0:T(1024)(128)(4,1)} %bitcast.16), calls=%async_computation.2 | async-start | bytes 1835008
Sparse Core Ops, SparseCore 0:
  22.3 146.1 all-reduce.1

commit v4 on v3

--- a/solution.py
+++ b/solution.py
@@ -75,8 +75,16 @@
         panel = p_ref[...]
         for part in range(0, n, BLOCK):
             cut = slice(part, part + BLOCK)
-            m_ref[:, cut] = m_ref[:, cut] - dot_nt(panel, p_ref[cut, :])
-            z_ref[:, cut] = z_ref[:, cut] - dot_nn(panel, z_ref[here, cut])
+            last = k == n // TILE - 1
+
+            @pl.when(jnp.logical_not(last) & (part + BLOCK > (k + 1) * TILE))
+            def _(cut=cut):
+                m_ref[:, cut] = m_ref[:, cut] - dot_nt(panel, p_ref[cut, :])
+
+            @pl.when(jnp.logical_not(last) & (part <= k * TILE))
+            def _(cut=cut):
+                z_ref[:, cut] = z_ref[:, cut] - dot_nn(panel, z_ref[here, cut])
+
         return carry
 
     lax.fori_loop(0, n // TILE, step, 0)

time: 213 us -> 213 us (level)
  Pallas kernels: 138 us -> 128 us
  waiting for transfers between devices: 1.42 us -> 11.1 us
    psum x1, waiting for transfers between devices: 1.4 us -> 11.1 us  [body(): listed = lax.psum(listed, 'row')]
    pallas_call x1, Pallas kernels: 66.8 us -> 57.1 us  [inverse_factor(): pl.pallas_call(invert_kernel, out_shape=jax.ShapeDtypeStruct((n, n), jnp....]
  transfers between devices with their start and end apart: 1 -> 1, of which waited for: 1 -> 1; matrix products, arithmetic and copies ran while one was open for 4% -> 4% of each run, Pallas kernels for 64% -> 59%
where the time goes in v4:
time: 213 us; the launch traced here: 212 us
  Pallas kernels  128 us (60%)
  matrix products  44.9 us (21%)
  between operations  16.1 us (8%)
  local copies, waits for them, and re-layouts  11.4 us (5%)
  waiting for transfers between devices  11.1 us (5%)
    pallas_call x1, Pallas kernels, sum_rows(): pl.pallas_call(functools.partial(sum_kernel, n), out_shape=jax.ShapeDtype...  68.5 us
    pallas_call x1, Pallas kernels, inverse_factor(): pl.pallas_call(invert_kernel, out_shape=jax.ShapeDtypeStruct((n, n), jnp....  57.1 us
    dot_general x1, matrix products, body(): update = weights - jnp.dot(left, middle, precision=split_mode)  24.7 us
    dot_general x1, matrix products, body(): middle = jnp.dot(inverse, listed, precision=split_mode)  11.7 us
    psum x1, waiting for transfers between devices, body(): listed = lax.psum(listed, 'row')  11.1 us
    unnamed x13, local copies, waits for them, and re-layouts  9.67 us
    dot_general x1, matrix products, body(): lax.dot_general(panels, inverse, (((1,), (1,)), ((), ())), precision=spli...  8.5 us
  transfers between devices with their start and end apart: 1, of which 1 were waited for; matrix products, arithmetic and copies ran while one was open for 4% of the time, Pallas kernels for 59%

profile of v4, /device:TPU:0, one launch (start us, length us, event | category | flops | bytes accessed | tf_op | source)
XLA Modules:
  0.0 212.5 jit_solution(10267275415132574672)
XLA Ops:
  7.2 0.0 all-reduce.2.cloned.1.call-start
  7.2 1.3 fusion.6
  10.4 0.1 pad_add_fusion.starts_ref
  10.5 0.0 copy-start.2
  10.5 2.4 %copy-done.2 = f32[1664,768]{1,0:T(8,128)S(1)} copy-done((f32[1664,768]{1,0:T(8,128)S(1)}, f32[1664,768]{1,0:T(8,128)}, u32[]{:S(2)}) %copy-start.2) | copy-done | bytes 5111832
  13.0 0.9 shard_map.50.x_ref
  13.9 0.0 copy-start.1
  13.9 4.4 %copy-done.1 = f32[1664,1792]{1,0:T(8,128)S(1)} copy-done((f32[1664,1792]{1,0:T(8,128)S(1)}, f32[1664,1792]{1,0:T(8,128)}, u32[]{:S(2)}) %copy-start.1) | copy-done | bytes 11927576
  18.3 1.5 shard_map.51
  19.7 0.0 copy-start
  19.8 2.4 %copy-done = f32[768,1792]{1,0:T(8,128)} copy-done((f32[768,1792]{1,0:T(8,128)}, f32[768,1792]{1,0:T(8,128)S(1)}, u32[]{:S(2)}) %copy-start) | copy-done | bytes 5505048
  22.2 0.0 all-reduce.2.cloned.1.call-update
  22.2 68.5 %shard_map.52 = f32[1536,256]{1,0:T(8,128)S(1)} custom-call(f32[1536,256]{1,0:T(8,128)S(1)} %shard_map.50.x_ref), custom_call_target="tpu_custom_call" | custom-call | flops 40000000000 | bytes 3145728 | tf_op jit(solution)/shard_map/pallas_call | solution.py:191
  90.8 0.1 fusion.5
  90.9 0.1 copy.15
  91.0 0.1 copy.17
  91.2 0.1 pad_maximum_fusion
  91.2 0.3 copy.14
  91.5 0.1 copy.16
  91.7 0.0 slice-start
  91.7 0.2 maximum_maximum_fusion.c_ref
  91.8 0.0 slice-start.1
  91.9 57.1 %shard_map.53 = f32[768,768]{1,0:T(8,128)S(1)} custom-call(f32[768,768]{1,0:T(8,128)S(1)} %maximum_maximum_fusion.c_ref), custom_call_target="tpu_custom_call" | custom-call | flops 40000000000 | bytes 4718592 | tf_op jit(solution)/shard_map/pallas_call | solution.py:95
  149.0 0.0 slice-done
  149.0 0.0 slice-done.1
  149.0 8.5 %fusion.7 = f32[768,1664]{1,0:T(8,128)} fusion(f32[768,768]{1,0:T(8,128)S(1)} %shard_map.53, f32[1664,768]{1,0:T(8,128)S(1)} %bitcast.17), kind=kOutput, calls=%fused_computation.20 | convolution fusion | flops 5888802816 | bytes 12582912 | tf_op jit(solution)/shard_map/dot_general | solution.py:227
  157.5 11.1 %all-reduce.2.cloned.1.call-done = f32[768,1792]{1,0:T(8,128)} async-done(((f32[768,1792]{1,0:T(8,128)}), f32[768,1792]{1,0:T(8,128)}) %all-reduce.2.cloned.1.call-update) | async-done | bytes 5505040 | tf_op jit(solution)/shard_map/psum | solution.py:215
  168.6 11.7 %multiply_reduce_fusion = (f32[768]{0:T(1024)S(1)}, f32[768,1792]{1,0:T(8,128)}) fusion(f32[768,768]{1,0:T(8,128)S(1)} %shard_map.53, f32[768,1792]{1,0:T(8,128)} %all-reduce.2.cloned.1.call-done), kind=kOutput, calls=%fused_computation.1 | convolution fusion | flops 6344539136 | bytes 13372416 | tf_op jit(solution)/shard_map/dot_general | solution.py:228
  180.3 0.1 reduce_sum.18
  180.4 0.5 broadcast_multiply_fusion
  180.9 24.7 %subtract_select_fusion = f32[1664,1792]{1,0:T(8,128)} fusion(f32[1664,1792]{1,0:T(8,128)} %x_ref.3, f32[768,1664]{1,0:T(8,128)} %fusion.7, f32[768,1792]{1,0:T(8,128)} %get-tuple-element.17, pred[1664]{0:T(1024)(128)(4,1)S(1)} %fusion.2), kind=kOutput, calls=%fused_computation | convolution fusion | flops 13746503680 | bytes 34473600 | tf_op jit(solution)/shard_map/dot_general | solution.py:234
  (3 shorter events, 0.0 us)
Async XLA Ops:
  7.2 161.4 %all-reduce.2.cloned.1.call-start = ((), (), s32[]{:S(2)}) async-start(), calls=%async_computation | async-start | bytes 11010048 | tf_op jit(solution)/shard_map/psum | solution.py:215
  10.5 2.5 %copy-start.2 = (f32[1664,768]{1,0:T(8,128)S(1)}, f32[1664,768]{1,0:T(8,128)}, u32[]{:S(2)}) copy-start(f32[1664,768]{1,0:T(8,128)} %x_ref.2) | copy-start | bytes 15335428
  13.9 4.4 %copy-start.1 = (f32[1664,1792]{1,0:T(8,128)S(1)}, f32[1664,1792]{1,0:T(8,128)}, u32[]{:S(2)}) copy-start(f32[1664,1792]{1,0:T(8,128)} %x_ref.3) | copy-start | bytes 35782660
  19.7 2.4 %copy-start = (f32[768,1792]{1,0:T(8,128)}, f32[768,1792]{1,0:T(8,128)S(1)}, u32[]{:S(2)}) copy-start(f32[768,1792]{1,0:T(8,128)S(1)} %shard_map.51) | copy-start | bytes 16515076
  91.7 57.3 %slice-start = ((s8[5111808]{0:T(1024)(128)(4,1)}), s8[4194304]{0:T(1024)(128)(4,1)S(1)}, s32[]{:S(2)}) async-start(s8[5111808]{0:T(1024)(128)(4,1)} %bitcast.16), calls=%async_computation.1 | async-start | bytes 8388608
  91.8 57.1 %slice-start.1 = ((s8[5111808]{0:T(1024)(128)(4,1)}), s8[917504]{0:T(1024)(128)(4,1)S(1)}, s32[]{:S(2)}) async-start(s8[5111808]{0:T(1024)(128)(4,1)} %bitcast.16), calls=%async_computation.2 | async-start | bytes 1835008
Sparse Core Ops, SparseCore 0:
  22.3 146.2 all-reduce.1
